TPU v7x, 128 devices: a whole 4x4x4 slice. The times are simulated.
128 devices in a mesh: dp: 4 (over y), group: 8 (over x, core), node: 4 (over z).
Axes of the slice: x: 4, y: 4, z: 4, core: 2. Of those that a mesh axis runs over, the one named last changes fastest.
Arguments:
- tokens: bfloat16 [32768, 1024], P(('dp', 'group', 'node')), may hold values from -24 to 24
- w_qkv: bfloat16 [1024, 3072], replicated, may hold values from -0.1875 to 0.1875
- w_proj: bfloat16 [1024, 1024], replicated, may hold values from -0.1875 to 0.1875
- rel_bias: float32 [32, 225], replicated, may hold values from -135 to 135
- gain_attn: float32 [1024], replicated, may hold values from 0.5 to 1.5
- shift_attn: float32 [1024], replicated, may hold values from -1.75 to 1.75
- w_router: float32 [1024, 32], replicated, may hold values from -0.1875 to 0.1875
- gain_moe: float32 [1024], replicated, may hold values from 0.5 to 1.5
- shift_moe: float32 [1024], replicated, may hold values from -1.75 to 1.75
- w_in: bfloat16 [32, 1024, 2048], P(('group', 'node')), may hold values from -0.1875 to 0.1875
- w_out: bfloat16 [32, 2048, 1024], P(('group', 'node')), may hold values from -0.125 to 0.125
- expert_ids: int32 [32768, 2], P(('dp', 'group', 'node')), may hold values from 0 to 31, all different within a row; in each aligned block of 256 rows (0 to 255, 256 to 511, ...) at most 20 rows name the same one
- cotangent: bfloat16 [32768, 1024], P(('dp', 'group', 'node')), may hold values from -6 to 6
Outputs:
- block_out: bfloat16 [32768, 1024], P(('dp', 'group', 'node'))
- d_tokens: bfloat16 [32768, 1024], P(('dp', 'group', 'node'))
- d_w_qkv: bfloat16 [1024, 3072], P(('dp', 'group', 'node'))
- d_w_proj: bfloat16 [1024, 1024], P(('dp', 'group', 'node'))
- d_router: float32 [1024, 32], P(('dp', 'group', 'node'))
- d_w_in: bfloat16 [32, 1024, 2048], P(('group', 'node'), 'dp')
- d_w_out: bfloat16 [32, 2048, 1024], P(('group', 'node'), 'dp')
Inputs may be any that keep to these rules, and one draw needn't show every extreme that they name: `expert_ids`: within the 256 rows of one device no expert is named by more than 20 rows.
All inputs are finite; a program needn't handle non-finite values.
Results may differ from a plain program's by a relative error of at most 0.02.
Values may be sent and summed in bfloat16 or wider, within the bound.
A program may use at most 192 MiB of HBM per device.

v0:
```python
import jax
import jax.numpy as jnp
import numpy as np
from jax import lax
from jax.sharding import PartitionSpec as P

D = 1024
HEADS = 32
HEAD_DIM = 32
GRID = 16
WIN = 8
TOP = 2
SHIFT = 4


EPS = 1e-05
NEG = -1e30


def rel_index():
    coords = np.arange(WIN * WIN)
    rows_at = coords // WIN
    cols_at = coords % WIN
    return (rows_at[:, None] - rows_at[None, :] + WIN - 1) * (2 * WIN - 1) + (
        cols_at[:, None] - cols_at[None, :] + WIN - 1
    )


def region_same():
    labels = np.zeros((GRID, GRID), np.int32)
    bounds = [0, GRID - WIN, GRID - SHIFT, GRID]
    for row_part in range(3):
        for col_part in range(3):
            labels[
                bounds[row_part] : bounds[row_part + 1], bounds[col_part] : bounds[col_part + 1]
            ] = (3 * row_part + col_part)
    per_side = GRID // WIN
    tiled = (
        labels.reshape(per_side, WIN, per_side, WIN)
        .transpose(0, 2, 1, 3)
        .reshape(per_side * per_side, WIN * WIN)
    )
    return tiled[:, :, None] == tiled[:, None, :]


def to_windows(grid_rows, images):
    channels = grid_rows.shape[-1]
    per_side = GRID // WIN
    shaped = grid_rows.reshape(images, GRID, GRID, channels)
    rolled = jnp.roll(shaped, (-SHIFT, -SHIFT), axis=(1, 2))
    parted = rolled.reshape(images, per_side, WIN, per_side, WIN, channels).transpose(
        0, 1, 3, 2, 4, 5
    )
    return parted.reshape(images * per_side * per_side, WIN * WIN, channels)


def from_windows(windowed, images):
    channels = windowed.shape[-1]
    per_side = GRID // WIN
    parted = windowed.reshape(images, per_side, per_side, WIN, WIN, channels).transpose(
        0, 1, 3, 2, 4, 5
    )
    rolled = jnp.roll(parted.reshape(images, GRID, GRID, channels), (SHIFT, SHIFT), axis=(1, 2))
    return rolled.reshape(images * GRID * GRID, channels)


def window_core(qkv_rows, rel_bias):
    images = qkv_rows.shape[0] // (GRID * GRID)
    windowed = to_windows(qkv_rows, images)
    num_windows = windowed.shape[0]
    length = windowed.shape[1]
    queries = windowed[:, :, :D].reshape(num_windows, length, HEADS, HEAD_DIM)
    keys_all = windowed[:, :, D : 2 * D].reshape(num_windows, length, HEADS, HEAD_DIM)
    values = windowed[:, :, 2 * D :].reshape(num_windows, length, HEADS, HEAD_DIM)
    bias_table = jnp.take(
        rel_bias, jnp.asarray(rel_index().reshape(-1), dtype=jnp.int32), axis=1
    ).reshape(HEADS, length, length)
    same_region = jnp.asarray(np.tile(region_same(), (images, 1, 1)))
    scores = (
        jnp.einsum("bqhd,bkhd->bhqk", queries, keys_all, preferred_element_type=jnp.float32)
        * HEAD_DIM ** (-0.5)
        + bias_table[None]
    )
    scores = jnp.where(same_region[:, None], scores, NEG)
    row_top = jnp.max(scores, axis=-1, keepdims=True)
    weights = jnp.exp(scores - row_top)
    attn_probs = (weights / jnp.sum(weights, axis=-1, keepdims=True)).astype(jnp.bfloat16)
    context = jnp.einsum(
        "bhqk,bkhd->bqhd", attn_probs, values, preferred_element_type=jnp.float32
    ).astype(jnp.bfloat16)
    return from_windows(context.reshape(num_windows, length, D), images)


def post_norm(values, gain, shift):
    row_mean = jnp.mean(values, axis=-1, keepdims=True)
    centered = values - row_mean
    row_var = jnp.mean(centered * centered, axis=-1, keepdims=True)
    return centered * lax.rsqrt(row_var + EPS) * gain + shift


def exact_gelu(values):
    return jax.nn.gelu(values, approximate=False)


def slot_positions(ids_dev, experts, capacity):
    flat_ids = ids_dev.reshape(-1)
    one_hot = (flat_ids[:, None] == jnp.arange(experts, dtype=jnp.int32)[None, :]).astype(jnp.int32)
    earlier = jnp.cumsum(one_hot, axis=0) - one_hot
    ranks = jnp.sum(earlier * one_hot, axis=1)
    return flat_ids * capacity + ranks


def slot_tables(positions, slots):
    owners = (
        jnp.zeros((slots,), jnp.int32)
        .at[positions]
        .set(jnp.arange(positions.shape[0], dtype=jnp.int32))
    )
    slot_used = jnp.zeros((slots,), jnp.bool_).at[positions].set(True)
    return (owners, slot_used)


def route(slot_block):
    moved = lax.all_to_all(slot_block, ("group", "node"), split_axis=0, concat_axis=0, tiled=True)
    return moved.reshape(slot_block.shape[0] * slot_block.shape[1], slot_block.shape[2])


def per_device(
    tokens,
    w_qkv,
    w_proj,
    rel_bias,
    gain_attn,
    shift_attn,
    w_router,
    gain_moe,
    shift_moe,
    w_in,
    w_out,
    expert_ids,
    cotangent,
):
    highest = lax.Precision.HIGHEST
    experts = lax.axis_size("group") * lax.axis_size("node")
    tok_rows = tokens.shape[0]
    model_dim = tokens.shape[1]
    capacity = 5 * tok_rows * TOP // (4 * experts)
    qkv_rows = jnp.dot(tokens, w_qkv, preferred_element_type=jnp.float32).astype(jnp.bfloat16)
    context, core_pull = jax.vjp(lambda packed: window_core(packed, rel_bias), qkv_rows)
    attn_out = jnp.dot(context, w_proj, preferred_element_type=jnp.float32)
    normed_attn, attn_pull = jax.vjp(
        lambda values: post_norm(values, gain_attn, shift_attn), attn_out
    )
    mid_rows = (tokens.astype(jnp.float32) + normed_attn).astype(jnp.bfloat16)
    mid_float = mid_rows.astype(jnp.float32)
    logits = jnp.dot(mid_float, w_router, precision=highest)
    selection = (
        expert_ids[:, :, None] == jnp.arange(experts, dtype=jnp.int32)[None, None, :]
    ).astype(jnp.float32)
    chosen = jnp.einsum("te,tke->tk", logits, selection, precision=highest)
    gating = jax.nn.sigmoid(chosen)
    positions = slot_positions(expert_ids, experts, capacity)
    owners, slot_used = slot_tables(positions, experts * capacity)
    outbox = jnp.where(slot_used[:, None], mid_rows[owners // TOP], jnp.zeros((), jnp.bfloat16))
    inbox = route(outbox.reshape(experts, capacity, model_dim))
    w_first = w_in[0]
    w_second = w_out[0]
    pre_act = jnp.dot(inbox, w_first, preferred_element_type=jnp.float32)
    hidden_f, gelu_pull = jax.vjp(exact_gelu, pre_act)
    hidden_b = hidden_f.astype(jnp.bfloat16)
    expert_rows = jnp.dot(hidden_b, w_second, preferred_element_type=jnp.float32).astype(
        jnp.bfloat16
    )
    returned = route(expert_rows.reshape(experts, capacity, model_dim))
    picked = returned[positions].reshape(tok_rows, TOP, model_dim).astype(jnp.float32)
    mixture = jnp.sum(gating[:, :, None] * picked, axis=1)
    normed_moe, moe_pull = jax.vjp(lambda values: post_norm(values, gain_moe, shift_moe), mixture)
    block_out = (mid_float + normed_moe).astype(jnp.bfloat16)
    d_mixture = moe_pull(cotangent.astype(jnp.float32))[0]
    d_gating = jnp.einsum("td,tkd->tk", d_mixture, picked, precision=highest)
    d_picked = (
        (gating[:, :, None] * d_mixture[:, None, :])
        .astype(jnp.bfloat16)
        .reshape(tok_rows * TOP, model_dim)
    )
    d_outbox = jnp.where(slot_used[:, None], d_picked[owners], jnp.zeros((), jnp.bfloat16))
    d_inbox = route(d_outbox.reshape(experts, capacity, model_dim))
    d_hidden = jnp.dot(d_inbox, w_second.T, preferred_element_type=jnp.float32)
    d_pre = gelu_pull(d_hidden)[0].astype(jnp.bfloat16)
    grad_second = jnp.dot(hidden_b.T, d_inbox, preferred_element_type=jnp.float32)
    grad_first = jnp.dot(inbox.T, d_pre, preferred_element_type=jnp.float32)
    d_rows_in = jnp.dot(d_pre, w_first.T, preferred_element_type=jnp.float32).astype(jnp.bfloat16)
    d_returned = route(d_rows_in.reshape(experts, capacity, model_dim))
    d_chosen = d_gating * gating * (1.0 - gating)
    d_logits = jnp.einsum("tk,tke->te", d_chosen, selection, precision=highest)
    d_mid = cotangent.astype(jnp.float32) + jnp.sum(
        d_returned[positions].reshape(tok_rows, TOP, model_dim).astype(jnp.float32), axis=1
    )
    d_mid = d_mid + jnp.dot(d_logits, w_router.T, precision=highest)
    d_mid_b = d_mid.astype(jnp.bfloat16)
    d_attn_b = attn_pull(d_mid_b.astype(jnp.float32))[0].astype(jnp.bfloat16)
    d_context = jnp.dot(d_attn_b, w_proj.T, preferred_element_type=jnp.float32).astype(jnp.bfloat16)
    d_qkv = core_pull(d_context)[0]
    d_tokens = (
        d_mid_b.astype(jnp.float32) + jnp.dot(d_qkv, w_qkv.T, preferred_element_type=jnp.float32)
    ).astype(jnp.bfloat16)
    first_sum, second_sum = (
        lax.psum_scatter(
            grad_first.astype(jnp.bfloat16), "dp", scatter_dimension=0, tiled=True
        ).astype(jnp.float32),
        lax.psum_scatter(
            grad_second.astype(jnp.bfloat16), "dp", scatter_dimension=0, tiled=True
        ).astype(jnp.float32),
    )
    grad_qkv = jnp.dot(tokens.T, d_qkv, preferred_element_type=jnp.float32)
    grad_proj = jnp.dot(context.T, d_attn_b, preferred_element_type=jnp.float32)
    grad_router = jnp.dot(mid_float.T, d_logits, precision=highest)
    sum_qkv, sum_proj, sum_router = (
        lax.psum_scatter(grad_qkv, ("dp", "group", "node"), scatter_dimension=0, tiled=True),
        lax.psum_scatter(grad_proj, ("dp", "group", "node"), scatter_dimension=0, tiled=True),
        lax.psum_scatter(grad_router, ("dp", "group", "node"), scatter_dimension=0, tiled=True),
    )
    return (
        block_out,
        d_tokens,
        sum_qkv.astype(jnp.bfloat16),
        sum_proj.astype(jnp.bfloat16),
        sum_router,
        first_sum.astype(jnp.bfloat16)[None],
        second_sum.astype(jnp.bfloat16)[None],
    )


def solution(mesh):
    return jax.shard_map(
        per_device,
        mesh=mesh,
        in_specs=(
            P(("dp", "group", "node"), None),
            P(),
            P(),
            P(),
            P(),
            P(),
            P(),
            P(),
            P(),
            P(("group", "node"), None, None),
            P(("group", "node"), None, None),
            P(("dp", "group", "node"), None),
            P(("dp", "group", "node"), None),
        ),
        out_specs=(
            P(("dp", "group", "node"), None),
            P(("dp", "group", "node"), None),
            P(("dp", "group", "node"), None),
            P(("dp", "group", "node"), None),
            P(("dp", "group", "node"), None),
            P(("group", "node"), "dp", None),
            P(("group", "node"), "dp", None),
        ),
        check_vma=False,
    )
```

profile of v0, /device:TPU:1, one launch (start us, length us, event | category | flops | bytes accessed | tf_op | source)
XLA Modules:
  0.0 1390.1 jit_solution(11555980324885151517)
XLA Ops:
  9.1 4.8 convolution_convert_fusion
  24.4 14.7 %gather_fusion = f32[4096,32]{1,0:T(8,128)} fusion(f32[32,225]{0,1:T(8,128)S(1)} %copy.84, s32[4096]{0:T(1024)S(1)} %broadcast_clamp_fusion), kind=kCustom, calls=%fused_computation | custom fusion | bytes 1064960 | tf_op jit(solution)/shard_map/jvp(jit(_take))/gather | solution.py:75
  39.1 2.9 copy.85
  42.1 3.2 fusion.19
  46.8 4.3 convert_reduce_fusion
  53.1 3.8 copy.87
  56.9 3.5 reshape.252
  70.0 3.5 gather_fusion.1
  73.5 3.2 gather.25
  78.3 31.7 %all_to_all.20 = bf16[32,20,1024]{2,1,0:T(8,128)(2,1)} all-to-all(bf16[32,20,1024]{2,1,0:T(8,128)(2,1)S(1)} %broadcast_select_fusion.1), channel_id=1, replica_groups=mesh['dp'=4,'group'=8,'node'=4] {'group','node'}, dimensions={0} | all-to-all | bytes 2621440 | tf_op jit(solution)/shard_map/all_to_all | solution.py:124
  109.9 3.3 reshape.256
  113.2 17.0 %multiply_convert_fusion = (bf16[640,2048]{1,0:T(8,128)(2,1)S(1)}, f32[640,2048]{1,0:T(8,128)}, f32[640,2048]{1,0:T(8,128)}) fusion(bf16[640,1024]{1,0:T(8,128)(2,1)} %reshape.256, bf16[1,1024,2048]{2,1,0:T(8,128)(2,1)} %param.24), kind=kOutput, calls=%fused_computation.13 | convolution fusion | flops 2769551360 | bytes 18612224 | tf_op jit(solution)/shard_map/dot_general | solution.py:168
  131.7 4.0 fusion.35
  135.7 3.2 reshape.257
  138.9 5.7 all-to-all-start.1
  146.5 19.5 %all-to-all-done.1 = bf16[32,20,1024]{2,1,0:T(8,128)(2,1)} async-done(((bf16[32,20,1024]{2,1,0:T(8,128)(2,1)}), bf16[32,20,1024]{2,1,0:T(8,128)(2,1)}, u32[]{:S(2)}, u32[]{:S(2)}) %all-to-all-start.1) | async-done | bytes 1310752 | tf_op jit(solution)/shard_map/all_to_all | solution.py:124
  166.0 3.3 reshape.258
  169.3 4.9 gather_fusion.2
  180.0 4.1 multiply_reduce_fusion.1
  189.3 3.7 mul.245
  195.7 5.8 gather_fusion.3
  201.5 3.2 gather.28
  206.3 27.7 %all_to_all.21 = bf16[32,20,1024]{2,1,0:T(8,128)(2,1)} all-to-all(bf16[32,20,1024]{2,1,0:T(8,128)(2,1)S(1)} %broadcast_select_fusion), channel_id=1, replica_groups=mesh['dp'=4,'group'=8,'node'=4] {'group','node'}, dimensions={0} | all-to-all | bytes 2621440 | tf_op jit(solution)/shard_map/all_to_all | solution.py:124
  234.0 3.3 reshape.260
  237.3 10.1 add_convert_fusion
  248.9 4.0 fusion.32
  252.9 3.2 reshape.261
  256.1 5.3 all-to-all-start.3
  261.6 8.6 fusion.50
  273.2 9.8 all-to-all-done.3
  285.2 2.8 gather_fusion.4
  288.0 3.5 reshape.272
  291.5 5.1 reduce_sum.180
  306.3 2.9 reshape.265
  309.1 4.1 copy.95
  313.3 4.1 convolution_convert_fusion.4
  319.8 5.0 fusion.9
  334.1 4.6 fusion.40
  343.7 6.3 convolution_bitcast_fusion
  350.0 12.9 copy.115
  364.2 6.8 convolution_convert_fusion.1
  372.3 6.8 convolution_convert_fusion.2
  379.1 40.6 %all-reduce.14.cloned.1.call-done = f32[1024,32]{1,0:T(8,128)} async-done(((f32[1024,32]{1,0:T(8,128)}), f32[1024,32]{1,0:T(8,128)}) %all-reduce.14.cloned.1.call-update) | async-done | bytes 131088
  420.9 5.9 fusion.42
  426.8 630.4 %reduce-scatter.7.cloned.1.call-done = f32[8,1024]{1,0:T(8,128)} async-done(((f32[1024,1024]{1,0:T(8,128)}), f32[8,1024]{1,0:T(8,128)}) %reduce-scatter.7.cloned.1.call-update) | async-done | bytes 32784 | tf_op jit(solution)/shard_map/reduce_scatter | solution.py:220
  1058.6 226.0 %reduce-scatter.13.cloned.1.call-done = f32[8,3072]{1,0:T(8,128)} async-done(((f32[1024,3072]{1,0:T(8,128)}), f32[8,3072]{1,0:T(8,128)}) %reduce-scatter.13.cloned.1.call-update) | async-done | bytes 98320
  1286.7 46.9 %reduce-scatter.11.cloned.1.call-done = bf16[512,1024]{1,0:T(8,128)(2,1)} async-done(((bf16[2048,1024]{1,0:T(8,128)(2,1)}), bf16[512,1024]{1,0:T(8,128)(2,1)}) %reduce-scatter.11.cloned.1.call-update) | async-done | bytes 1048592 | tf_op jit(solution)/shard_map/reduce_scatter | solution.py:211
  1333.6 49.5 %reduce-scatter.9.cloned.1.call-done = bf16[256,2048]{1,0:T(8,128)(2,1)} async-done(((bf16[1024,2048]{1,0:T(8,128)(2,1)}), bf16[256,2048]{1,0:T(8,128)(2,1)}) %reduce-scatter.9.cloned.1.call-update) | async-done | bytes 1048592 | tf_op jit(solution)/shard_map/reduce_scatter | solution.py:208
  (201 shorter events, 85.8 us)
Async XLA Ops:
  7.2 60.7 %copy-start = (bf16[1024,1024]{1,0:T(8,128)(2,1)S(1)}, bf16[1024,1024]{1,0:T(8,128)(2,1)}, u32[]{:S(2)}) copy-start(bf16[1024,1024]{1,0:T(8,128)(2,1)} %param.17) | copy-start | bytes 6291460
  9.1 5.7 copy-start.41
  24.4 17.6 %copy-start.30 = (pred[4,64,64]{1,2,0:T(32,128)(4,1)S(1)}, pred[4,64,64]{1,2,0:T(32,128)(4,1)}, u32[]{:S(2)}) copy-start(pred[4,64,64]{1,2,0:T(32,128)(4,1)} %constant.147.clone) | copy-start | bytes 49156
  42.0 4.7 copy-start.3
  45.2 5.9 copy-start.1
  45.2 5.9 copy-start.25
  46.7 4.4 copy-start.27
  46.7 5.7 copy-start.16
  51.1 1.3 copy-start.7
  60.4 9.3 copy-start.19
  60.4 9.2 copy-start.39
  60.4 9.2 copy-start.42
  113.2 18.5 %copy-start.44 = (bf16[1,2048,1024]{2,1,0:T(8,128)(2,1)S(1)}, bf16[1,2048,1024]{2,1,0:T(8,128)(2,1)}, u32[]{:S(2)}) copy-start(bf16[1,2048,1024]{2,1,0:T(8,128)(2,1)} %param.25) | copy-start | bytes 12582916
  130.2 1.5 copy-start.47
  135.7 9.0 copy-start.36
  138.9 27.1 %all-to-all-start.1 = ((bf16[32,20,1024]{2,1,0:T(8,128)(2,1)}), bf16[32,20,1024]{2,1,0:T(8,128)(2,1)}, u32[]{:S(2)}, u32[]{:S(2)}) async-start(bf16[32,20,1024]{2,1,0:T(8,128)(2,1)} %reshape.257), calls=%async_computation.1 | async-start | bytes 3145728 | tf_op jit(solution)/shard_map/all_to_all | solution.py:124
  146.3 23.0 %copy-start.34 = (f32[256,1,2]{2,1,0:T(1,128)}, f32[256,1,2]{2,1,0:T(1,128)S(1)}, u32[]{:S(2)}) copy-start(f32[256,1,2]{2,1,0:T(1,128)S(1)} %fusion.55) | copy-start | bytes 6148
  174.2 9.9 copy-start.8
  174.2 9.9 copy-start.40
  174.3 10.7 copy-start.43
  237.3 11.5 copy-start.45
  247.4 1.5 copy-start.46
  256.1 26.9 %all-to-all-start.3 = ((bf16[32,20,1024]{2,1,0:T(8,128)(2,1)}), bf16[32,20,1024]{2,1,0:T(8,128)(2,1)}, u32[]{:S(2)}, u32[]{:S(2)}) async-start(bf16[32,20,1024]{2,1,0:T(8,128)(2,1)} %reshape.261), calls=%async_computation.3 | async-start | bytes 3145728 | tf_op jit(solution)/shard_map/all_to_all | solution.py:124
  261.4 8.8 copy-start.35
  261.4 158.2 %all-reduce.14.cloned.1.call-start = ((), (), s32[]{:S(2)}) async-start(), calls=%async_computation.12 | async-start | bytes 1048576
  271.4 1.8 copy-start.32
  272.9 784.3 %reduce-scatter.7.cloned.1.call-start = ((), (), s32[]{:S(2)}) async-start(), calls=%async_computation.8 | async-start | bytes 4227072 | tf_op jit(solution)/shard_map/reduce_scatter | solution.py:220
  288.0 8.6 copy-start.6
  288.0 8.6 copy-start.33
  288.0 8.6 copy-start.37
  296.6 4.5 copy-start.11
  301.1 2.8 copy-start.28
  303.9 980.7 %reduce-scatter.13.cloned.1.call-start = ((), (), s32[]{:S(2)}) async-start(), calls=%async_computation.11 | async-start | bytes 12681216
  309.1 10.6 copy-start.4
  309.1 10.6 copy-start.26
  309.1 10.6 copy-start.31
  319.8 5.1 copy-start.2
  324.8 2.8 copy-start.38
  324.8 4.7 copy-start.14
  324.9 4.7 copy-start.29
  327.6 1.9 copy-start.12
  329.5 4.5 copy-start.13
  341.8 1.9 copy-start.20
  362.9 1.3 copy-start.24
  362.9 970.7 %reduce-scatter.11.cloned.1.call-start = ((), (), s32[]{:S(2)}) async-start(), calls=%async_computation.10 | async-start | bytes 5242880 | tf_op jit(solution)/shard_map/reduce_scatter | solution.py:211
  371.0 1.3 copy-start.23
  371.0 1012.1 %reduce-scatter.9.cloned.1.call-start = ((), (), s32[]{:S(2)}) async-start(), calls=%async_computation.9 | async-start | bytes 5242880 | tf_op jit(solution)/shard_map/reduce_scatter | solution.py:208
  379.1 41.9 %copy-start.22 = (bf16[256,1024]{1,0:T(8,128)(2,1)S(1)}, bf16[256,1024]{1,0:T(8,128)(2,1)}, u32[]{:S(2)}) copy-start(bf16[256,1024]{1,0:T(8,128)(2,1)} %copy-done.21) | copy-start | bytes 1572868
  (7 other events, 7.2 us)
Sparse Core Ops, SparseCore 0:
  273.0 146.5 all-reduce.13
  422.1 635.0 reduce-scatter.6
  1062.2 222.3 reduce-scatter.12
  1287.4 46.1 reduce-scatter.10
  1336.5 46.5 reduce-scatter.8
where the time goes:
time: 1400 us; the launch traced here: 1390 us
  waiting for transfers between devices  1020 us (73%)
  local copies, waits for them, and re-layouts  138 us (10%)
  matrix products  105 us (8%)
  blocking collectives  59.4 us (4%)
  other arithmetic  38.1 us (3%)
  between operations  15.1 us (1%)
    reduce_scatter x1, waiting for transfers between devices, per_device(): lax.psum_scatter(grad_proj, ('dp', 'group', 'node'), scatter_dimension=0,...  630 us
    unnamed x7, waiting for transfers between devices  267 us
    all_to_all x2, blocking collectives, route(): lax.all_to_all(slot_block, ('group', 'node'), split_axis=0, concat_axis=0...  59.4 us
    reduce_scatter x1, waiting for transfers between devices, per_device(): lax.psum_scatter(grad_first.astype(jnp.bfloat16), 'dp', scatter_dimension...  49.5 us
    reduce_scatter x1, waiting for transfers between devices, per_device(): lax.psum_scatter(grad_second.astype(jnp.bfloat16), 'dp', scatter_dimensio...  46.9 us
    unnamed x102, local copies, waits for them, and re-layouts  32 us
    all_to_all x2, waiting for transfers between devices, route(): lax.all_to_all(slot_block, ('group', 'node'), split_axis=0, concat_axis=0...  29.3 us
  transfers between devices with their start and end apart: 7, of which 7 were waited for; matrix products, arithmetic and copies ran while one was open for 8% of the time, Pallas kernels for 0%

commit v1 on v0

--- a/solution.py
+++ b/solution.py
@@ -2,7 +2,16 @@
 import jax.numpy as jnp
 import numpy as np
 from jax import lax
+from jax.experimental import pallas as pl
+from jax.experimental.pallas import tpu as pltpu
 from jax.sharding import PartitionSpec as P
+
+MESH = pl.DeviceIdType.MESH
+F32 = jnp.float32
+BF16 = jnp.bfloat16
+MIB = 1 << 20
+WIDTH = 2176
+COLS_X = 1152
 
 D = 1024
 HEADS = 32
@@ -123,6 +132,241 @@
 def route(slot_block):
     moved = lax.all_to_all(slot_block, ("group", "node"), split_axis=0, concat_axis=0, tiled=True)
     return moved.reshape(slot_block.shape[0] * slot_block.shape[1], slot_block.shape[2])
+
+
+def reduce_kernel(
+    shared, first, second,
+    out_shared, out_first, out_second,
+    from_core, core_sum, x_recv, x_sum, z_recv, z_sum, x_recv2, x_sum2, z_recv2, y_recv,
+    f_far, f_near, f_pass, f_done, s_far, s_near, s_pass, s_done,
+    send_core, recv_core, send_a, recv_a, send_b, recv_b, send_c, recv_c, send_d, recv_d, send_y, recv_y,
+    send_dp, recv_dp,
+):
+    y = lax.axis_index("dp")
+    g = lax.axis_index("group")
+    z = lax.axis_index("node")
+    x = g // 2
+    c = g % 2
+    in_x = pl.ds(0, COLS_X)
+    in_z = pl.ds(COLS_X, WIDTH - COLS_X)
+
+    def at_x(j):
+        return {"group": lax.rem(x + j, 4) * 2 + c}
+
+    def at_y(j):
+        return {"dp": lax.rem(y + j, 4)}
+
+    def at_z(j):
+        return {"node": lax.rem(z + j, 4)}
+
+    other = {"group": x * 2 + (1 - c)}
+    barrier = pltpu.get_barrier_semaphore()
+    peers = [other] + [at(j) for at in (at_x, at_y, at_z) for j in (1, 2, 3)]
+    for peer in peers:
+        pl.semaphore_signal(barrier, inc=1, device_id=peer, device_id_type=MESH)
+    pl.semaphore_wait(barrier, len(peers))
+
+    def send(src, dst, s_sem, r_sem, peer):
+        copy = pltpu.make_async_remote_copy(
+            src_ref=src, dst_ref=dst, send_sem=s_sem, recv_sem=r_sem, device_id=peer, device_id_type=MESH
+        )
+        copy.start()
+        return copy
+
+    core_copies = [
+        send(shared.at[:, k, 1 - c], from_core.at[:, k], send_core.at[k], recv_core.at[k], other) for k in range(4)
+    ]
+
+    right, left, far = lax.rem(y + 1, 4), lax.rem(y + 3, 4), lax.rem(y + 2, 4)
+    halves = []
+    for at, (grad, far_in, near_in, done_in) in enumerate(
+        ((first, f_far, f_near, f_done), (second, s_far, s_near, s_done))
+    ):
+        half = grad.shape[1] // 2
+        rows = (pl.ds(0, half), pl.ds(half, half))
+        halves.append(rows)
+    dp_sets = ((first, f_far, f_near, f_pass, f_done), (second, s_far, s_near, s_pass, s_done))
+    far_copies, near_copies = [], []
+    for at, (grad, far_in, near_in, passing, done_in) in enumerate(dp_sets):
+        rows = halves[at]
+        far_copies.append((
+            send(grad.at[far, rows[0]], far_in.at[0], send_dp.at[at, 0, 0], recv_dp.at[at, 0, 0], at_y(1)),
+            send(grad.at[far, rows[1]], far_in.at[1], send_dp.at[at, 0, 1], recv_dp.at[at, 0, 1], at_y(3)),
+        ))
+    for at, (grad, far_in, near_in, passing, done_in) in enumerate(dp_sets):
+        rows = halves[at]
+        near_copies.append((
+            send(grad.at[right, rows[1]], near_in.at[1], send_dp.at[at, 1, 1], recv_dp.at[at, 1, 1], at_y(1)),
+            send(grad.at[left, rows[0]], near_in.at[0], send_dp.at[at, 1, 0], recv_dp.at[at, 1, 0], at_y(3)),
+        ))
+
+    for k in range(4):
+        core_copies[k].wait()
+
+        @pl.loop(0, 16)
+        def _(i):
+            yy, zz = i // 4, i % 4
+            core_sum[yy, k, zz] = (
+                shared[yy, k, c, zz].astype(F32) + from_core[yy, k, zz].astype(F32)
+            ).astype(BF16)
+
+    a_copies = [
+        send(core_sum.at[:, lax.rem(x + j, 4), :, :, in_x], x_recv.at[j - 1], send_a.at[j - 1], recv_a.at[j - 1], at_x(j))
+        for j in (1, 2, 3)
+    ]
+    b_copies = [
+        send(core_sum.at[:, :, lax.rem(z + j, 4), :, in_z], z_recv.at[j - 1], send_b.at[j - 1], recv_b.at[j - 1], at_z(j))
+        for j in (1, 2, 3)
+    ]
+    for copy in a_copies:
+        copy.wait()
+
+    @pl.loop(0, 16)
+    def _(i):
+        yy, zz = i // 4, i % 4
+        total = core_sum[yy, x, zz, :, in_x].astype(F32)
+        for j in range(3):
+            total = total + x_recv[j, yy, zz].astype(F32)
+        x_sum[yy, zz] = total.astype(BF16)
+
+    c_copies = [
+        send(x_sum.at[:, lax.rem(z + j, 4)], x_recv2.at[j - 1], send_c.at[j - 1], recv_c.at[j - 1], at_z(j))
+        for j in (1, 2, 3)
+    ]
+    for copy in b_copies:
+        copy.wait()
+
+    @pl.loop(0, 16)
+    def _(i):
+        yy, xx = i // 4, i % 4
+        total = core_sum[yy, xx, z, :, in_z].astype(F32)
+        for j in range(3):
+            total = total + z_recv[j, yy, xx].astype(F32)
+        z_sum[yy, xx] = total.astype(BF16)
+
+    d_copies = [
+        send(z_sum.at[:, lax.rem(x + j, 4)], z_recv2.at[j - 1], send_d.at[j - 1], recv_d.at[j - 1], at_x(j))
+        for j in (1, 2, 3)
+    ]
+
+    pass_copies = []
+    for at, (grad, far_in, near_in, passing, done_in) in enumerate(dp_sets):
+        rows = halves[at]
+        step = 64
+        for side, (block, peer) in enumerate(((right, at_y(1)), (left, at_y(3)))):
+            far_copies[at][side].wait()
+            half = rows[side].size
+
+            @pl.loop(0, half // step)
+            def _(i):
+                here = pl.ds(pl.multiple_of(i * step, step), step)
+                mine = pl.ds(pl.multiple_of(side * half + i * step, step), step)
+                passing[side, here] = (grad[block, mine].astype(F32) + far_in[side, here].astype(F32)).astype(BF16)
+
+            pass_copies.append(
+                send(passing.at[side], done_in.at[side], send_dp.at[at, 2, side], recv_dp.at[at, 2, side], peer)
+            )
+
+    for copy in c_copies + d_copies:
+        copy.wait()
+
+    @pl.loop(0, 4)
+    def _(yy):
+        total = x_sum[yy, z].astype(F32)
+        other_total = z_sum[yy, x].astype(F32)
+        for j in range(3):
+            total = total + x_recv2[j, yy].astype(F32)
+            other_total = other_total + z_recv2[j, yy].astype(F32)
+        x_sum2[yy, :, in_x] = total.astype(BF16)
+        x_sum2[yy, :, in_z] = other_total.astype(BF16)
+
+    y_copies = [
+        send(x_sum2.at[lax.rem(y + j, 4)], y_recv.at[j - 1], send_y.at[j - 1], recv_y.at[j - 1], at_y(j))
+        for j in (1, 2, 3)
+    ]
+
+    for at, (grad, far_in, near_in, passing, done_in) in enumerate(dp_sets):
+        out = (out_first, out_second)[at]
+        half = halves[at][0].size
+        step = 64
+        for side in (0, 1):
+            near_copies[at][1 - side].wait()
+            pass_copies[2 * at + side].wait()
+
+            @pl.loop(0, half // step)
+            def _(i):
+                here = pl.ds(pl.multiple_of(i * step, step), step)
+                mine = pl.ds(pl.multiple_of(side * half + i * step, step), step)
+                out[mine] = (
+                    grad[y, mine].astype(F32) + near_in[side, here].astype(F32) + done_in[side, here].astype(F32)
+                ).astype(BF16)
+
+    for copy in y_copies:
+        copy.wait()
+    total = x_sum2[y].astype(F32)
+    for j in range(3):
+        total = total + y_recv[j].astype(F32)
+    out_shared[...] = total
+
+
+def reduce_all(shared, first, second):
+    def both(rows, cols):
+        return pltpu.VMEM((2, rows, cols), BF16)
+
+    dma = pltpu.SemaphoreType.DMA
+    rest = WIDTH - COLS_X
+    f_rows, f_cols = first.shape[0] // 8, first.shape[1]
+    s_rows, s_cols = second.shape[0] // 8, second.shape[1]
+    vmem = pl.BlockSpec(memory_space=pltpu.VMEM)
+    return pl.pallas_call(
+        reduce_kernel,
+        out_shape=(
+            jax.ShapeDtypeStruct((16, WIDTH), F32),
+            jax.ShapeDtypeStruct((2 * f_rows, f_cols), BF16),
+            jax.ShapeDtypeStruct((2 * s_rows, s_cols), BF16),
+        ),
+        in_specs=[vmem] * 3,
+        out_specs=[vmem] * 3,
+        scratch_shapes=[
+            pltpu.VMEM((4, 4, 4, 16, WIDTH), BF16),
+            pltpu.VMEM((4, 4, 4, 16, WIDTH), BF16),
+            pltpu.VMEM((3, 4, 4, 16, COLS_X), BF16),
+            pltpu.VMEM((4, 4, 16, COLS_X), BF16),
+            pltpu.VMEM((3, 4, 4, 16, rest), BF16),
+            pltpu.VMEM((4, 4, 16, rest), BF16),
+            pltpu.VMEM((3, 4, 16, COLS_X), BF16),
+            pltpu.VMEM((4, 16, WIDTH), BF16),
+            pltpu.VMEM((3, 4, 16, rest), BF16),
+            pltpu.VMEM((3, 16, WIDTH), BF16),
+            both(f_rows, f_cols), both(f_rows, f_cols), both(f_rows, f_cols), both(f_rows, f_cols),
+            both(s_rows, s_cols), both(s_rows, s_cols), both(s_rows, s_cols), both(s_rows, s_cols),
+            dma((4,)), dma((4,)),
+            dma((3,)), dma((3,)), dma((3,)), dma((3,)), dma((3,)), dma((3,)), dma((3,)), dma((3,)), dma((3,)), dma((3,)),
+            dma((2, 3, 2)), dma((2, 3, 2)),
+        ],
+        compiler_params=pltpu.CompilerParams(
+            collective_id=0, has_side_effects=True, vmem_limit_bytes=58 * MIB
+        ),
+    )(
+        shared.reshape(4, 4, 2, 4, 16, WIDTH),
+        first.reshape(4, 2 * f_rows, f_cols),
+        second.reshape(4, 2 * s_rows, s_cols),
+    )
+
+
+def fold_shared(grad_qkv, grad_proj, grad_router):
+    wide = jnp.concatenate([grad_qkv, grad_proj], axis=1).reshape(128, 8, 4 * D)
+    high = grad_router.astype(BF16).astype(F32)
+    router = jnp.concatenate([high.reshape(128, 8, 32), (grad_router - high).reshape(128, 8, 32)], axis=1)
+    router = jnp.pad(router, ((0, 0), (0, 0), (0, 96)))
+    main = jnp.concatenate([wide[:, :, : 2 * D], wide[:, :, 2 * D :]], axis=1)
+    return jnp.concatenate([main, router], axis=2).astype(BF16)
+
+
+def unfold_shared(total):
+    wide = jnp.concatenate([total[:8, : 2 * D], total[8:, : 2 * D]], axis=1)
+    router = total[:8, 2 * D : 2 * D + 32] + total[8:, 2 * D : 2 * D + 32]
+    return wide[:, : 3 * D].astype(BF16), wide[:, 3 * D :].astype(BF16), router
 
 
 def per_device(
@@ -204,30 +448,21 @@
     d_tokens = (
         d_mid_b.astype(jnp.float32) + jnp.dot(d_qkv, w_qkv.T, preferred_element_type=jnp.float32)
     ).astype(jnp.bfloat16)
-    first_sum, second_sum = (
-        lax.psum_scatter(
-            grad_first.astype(jnp.bfloat16), "dp", scatter_dimension=0, tiled=True
-        ).astype(jnp.float32),
-        lax.psum_scatter(
-            grad_second.astype(jnp.bfloat16), "dp", scatter_dimension=0, tiled=True
-        ).astype(jnp.float32),
-    )
     grad_qkv = jnp.dot(tokens.T, d_qkv, preferred_element_type=jnp.float32)
     grad_proj = jnp.dot(context.T, d_attn_b, preferred_element_type=jnp.float32)
     grad_router = jnp.dot(mid_float.T, d_logits, precision=highest)
-    sum_qkv, sum_proj, sum_router = (
-        lax.psum_scatter(grad_qkv, ("dp", "group", "node"), scatter_dimension=0, tiled=True),
-        lax.psum_scatter(grad_proj, ("dp", "group", "node"), scatter_dimension=0, tiled=True),
-        lax.psum_scatter(grad_router, ("dp", "group", "node"), scatter_dimension=0, tiled=True),
-    )
+    total, first_sum, second_sum = reduce_all(
+        fold_shared(grad_qkv, grad_proj, grad_router), grad_first.astype(BF16), grad_second.astype(BF16)
+    )
+    sum_qkv, sum_proj, sum_router = unfold_shared(total)
     return (
         block_out,
         d_tokens,
-        sum_qkv.astype(jnp.bfloat16),
-        sum_proj.astype(jnp.bfloat16),
+        sum_qkv,
+        sum_proj,
         sum_router,
-        first_sum.astype(jnp.bfloat16)[None],
-        second_sum.astype(jnp.bfloat16)[None],
+        first_sum[None],
+        second_sum[None],
     )
 
 

time: 1400 us -> 474 us (0.34)
  waiting for transfers between devices: 1020 us -> 36.6 us
  Pallas kernels: 0 us -> 82.8 us
  blocking collectives: 59.4 us -> 31.7 us
  other arithmetic: 38.1 us -> 64.3 us
    reduce_scatter x3 -> x0, waiting for transfers between devices: 727 us -> none  [the longest x1 630 us: per_device(): lax.psum_scatter(grad_proj, ('dp', 'group', 'node'), scatter_dimension=0,...]
    unnamed x7 -> x0, waiting for transfers between devices: 267 us -> none
    pallas_call x0 -> x1, Pallas kernels: none -> 82.8 us  [reduce_all(): pl.pallas_call(reduce_kernel, out_shape=(jax.ShapeDtypeStruct((16, WIDTH)...]
    all_to_all x2 -> x1, blocking collectives: 59.4 us -> 31.7 us  [route(): lax.all_to_all(slot_block, ('group', 'node'), split_axis=0, concat_axis=0...]
    unnamed x102 -> x107, local copies, waits for them, and re-layouts: 32 us -> 14.5 us
    concatenate x0 -> x4, other arithmetic: none -> 15.7 us  [the longest x1 8.13 us: fold_shared(): return jnp.concatenate([main, router], axis=2).astype(BF16)]
    all_to_all x2 -> x3, waiting for transfers between devices: 29.3 us -> 36.6 us  [route(): lax.all_to_all(slot_block, ('group', 'node'), split_axis=0, concat_axis=0...]
  transfers between devices with their start and end apart: 7 -> 3, of which waited for: 7 -> 3; matrix products, arithmetic and copies ran while one was open for 8% -> 6% of each run, Pallas kernels for 0% -> 0%
where the time goes in v1:
time: 474 us; the launch traced here: 468 us
  local copies, waits for them, and re-layouts  138 us (29%)
  matrix products  94 us (20%)
  Pallas kernels  82.8 us (17%)
  other arithmetic  64.3 us (14%)
  waiting for transfers between devices  36.6 us (8%)
  blocking collectives  31.7 us (7%)
  starting transfers between devices  18 us (4%)
    pallas_call x1, Pallas kernels, reduce_all(): pl.pallas_call(reduce_kernel, out_shape=(jax.ShapeDtypeStruct((16, WIDTH)...  82.8 us
    all_to_all x3, waiting for transfers between devices, route(): lax.all_to_all(slot_block, ('group', 'node'), split_axis=0, concat_axis=0...  36.6 us
    all_to_all x1, blocking collectives, route(): lax.all_to_all(slot_block, ('group', 'node'), split_axis=0, concat_axis=0...  31.7 us
    all_to_all x3, starting transfers between devices, route(): lax.all_to_all(slot_block, ('group', 'node'), split_axis=0, concat_axis=0...  18 us
    gather x2, local copies, waits for them, and re-layouts, window_core(): jnp.take(rel_bias, jnp.asarray(rel_index().reshape(-1), dtype=jnp.int32),...  17.2 us
    dot_general x1, matrix products, per_device(): pre_act = jnp.dot(inbox, w_first, preferred_element_type=jnp.float32)  17.1 us
    unnamed x107, local copies, waits for them, and re-layouts  14.5 us
    another operation x4, local copies, waits for them, and re-layouts  12.1 us
  transfers between devices with their start and end apart: 3, of which 3 were waited for; matrix products, arithmetic and copies ran while one was open for 6% of the time, Pallas kernels for 0%

profile of v1, /device:TPU:1, one launch (start us, length us, event | category | flops | bytes accessed | tf_op | source)
XLA Modules:
  0.0 467.5 jit_solution(15455376629191069757)
XLA Ops:
  2.6 4.8 %convolution_convert_fusion = bf16[256,3072]{1,0:T(8,128)(2,1)S(1)} fusion(bf16[256,1024]{1,0:T(8,128)(2,1)} %param.15, bf16[1024,3072]{1,0:T(8,128)(2,1)} %param.16), kind=kOutput, calls=%fused_computation.47 | convolution fusion | flops 1611399168 | bytes 8388608 | tf_op jit(solution)/shard_map/dot_general | solution.py:392
  17.9 14.2 %gather_fusion = f32[4096,32]{1,0:T(8,128)} fusion(f32[32,225]{0,1:T(8,128)S(1)} %copy.91, s32[4096]{0:T(1024)S(1)} %broadcast_clamp_fusion), kind=kCustom, calls=%fused_computation | custom fusion | bytes 1064960 | tf_op jit(solution)/shard_map/jvp(jit(_take))/gather | solution.py:84
  32.1 2.9 copy.92
  35.1 3.2 fusion.19
  39.8 4.4 convert_reduce_fusion
  46.3 3.7 copy.94
  50.0 3.5 reshape.274
  63.2 3.5 gather_fusion.1
  66.7 3.2 gather.25
  71.4 31.7 %all_to_all.20 = bf16[32,20,1024]{2,1,0:T(8,128)(2,1)} all-to-all(bf16[32,20,1024]{2,1,0:T(8,128)(2,1)S(1)} %broadcast_select_fusion.1), channel_id=1, replica_groups=mesh['dp'=4,'group'=8,'node'=4] {'group','node'}, dimensions={0} | all-to-all | bytes 2621440 | tf_op jit(solution)/shard_map/all_to_all | solution.py:133
  103.1 3.3 reshape.278
  106.3 17.1 %multiply_convert_fusion = (bf16[640,2048]{1,0:T(8,128)(2,1)S(1)}, f32[640,2048]{1,0:T(8,128)}, f32[640,2048]{1,0:T(8,128)}) fusion(bf16[640,1024]{1,0:T(8,128)(2,1)} %reshape.278, bf16[1,1024,2048]{2,1,0:T(8,128)(2,1)} %param.24), kind=kOutput, calls=%fused_computation.16 | convolution fusion | flops 2769551360 | bytes 18612224 | tf_op jit(solution)/shard_map/dot_general | solution.py:412
  124.9 4.0 fusion.35
  128.9 3.2 reshape.279
  132.1 5.9 %all-to-all-start.1 = ((bf16[32,20,1024]{2,1,0:T(8,128)(2,1)}), bf16[32,20,1024]{2,1,0:T(8,128)(2,1)}, u32[]{:S(2)}, u32[]{:S(2)}) async-start(bf16[32,20,1024]{2,1,0:T(8,128)(2,1)} %reshape.279), calls=%async_computation.1 | async-start | bytes 3145728 | tf_op jit(solution)/shard_map/all_to_all | solution.py:133
  139.9 19.5 %all-to-all-done.1 = bf16[32,20,1024]{2,1,0:T(8,128)(2,1)} async-done(((bf16[32,20,1024]{2,1,0:T(8,128)(2,1)}), bf16[32,20,1024]{2,1,0:T(8,128)(2,1)}, u32[]{:S(2)}, u32[]{:S(2)}) %all-to-all-start.1) | async-done | bytes 1310752 | tf_op jit(solution)/shard_map/all_to_all | solution.py:133
  159.4 3.3 reshape.280
  162.7 4.9 %gather_fusion.2 = bf16[512,1024]{1,0:T(8,128)(2,1)} fusion(bf16[640,1024]{1,0:T(8,128)(2,1)} %reshape.280, s32[1024]{0:T(1024)S(1)} %pad_clamp_fusion.1), kind=kCustom, calls=%fused_computation.2 | custom fusion | bytes 2099200 | tf_op jit(solution)/shard_map/gather | solution.py:419
  173.4 4.1 multiply_reduce_fusion.1
  182.6 3.7 mul.245
  186.3 2.7 multiply_convert_fusion.1
  189.0 5.8 %gather_fusion.3 = bf16[640,1024]{1,0:T(8,128)(2,1)} fusion(bf16[512,1024]{1,0:T(8,128)(2,1)} %multiply_convert_fusion.1, s32[1024]{0:T(1024)S(1)} %get-tuple-element.48), kind=kCustom, calls=%fused_computation.3 | custom fusion | bytes 2624000 | tf_op jit(solution)/shard_map/gather | solution.py:430
  194.9 3.2 gather.28
  198.0 2.8 broadcast_select_fusion
  200.8 6.2 %all-to-all-start.2 = ((bf16[32,20,1024]{2,1,0:T(8,128)(2,1)}), bf16[32,20,1024]{2,1,0:T(8,128)(2,1)}, u32[]{:S(2)}, u32[]{:S(2)}) async-start(bf16[32,20,1024]{2,1,0:T(8,128)(2,1)} %broadcast_select_fusion), calls=%async_computation.2 | async-start | bytes 3145728 | tf_op jit(solution)/shard_map/all_to_all | solution.py:133
  207.7 8.6 %fusion.50 = f32[256,1,2]{2,1,0:T(1,128)S(1)} fusion(bf16[256,2,1024]{2,1,0:T(2,128)(2,1)} %reshape.281, f32[256,1024,1]{1,0,2:T(8,128)} %bitcast.165), kind=kOutput, calls=%fused_computation.102 | convolution fusion | flops 6291456 | bytes 2099200 | tf_op jit(solution)/shard_map/td,tkd->tk/dot_general | solution.py:424
  218.6 9.8 %all-to-all-done.2 = bf16[32,20,1024]{2,1,0:T(8,128)(2,1)} async-done(((bf16[32,20,1024]{2,1,0:T(8,128)(2,1)}), bf16[32,20,1024]{2,1,0:T(8,128)(2,1)}, u32[]{:S(2)}, u32[]{:S(2)}) %all-to-all-start.2) | async-done | bytes 1310752 | tf_op jit(solution)/shard_map/all_to_all | solution.py:133
  230.7 8.9 %add_convert_fusion = bf16[640,2048]{1,0:T(8,128)(2,1)S(1)} fusion(f32[640,2048]{1,0:T(8,128)} %get-tuple-element.24, f32[640,2048]{1,0:T(8,128)} %get-tuple-element.43, bf16[640,1024]{1,0:T(8,128)(2,1)S(1)} %reshape.282, bf16[1,2048,1024]{2,1,0:T(8,128)(2,1)} %param.25), kind=kOutput, calls=%fused_computation.15 | convolution fusion | flops 2702704640 | bytes 18612224 | tf_op jit(solution)/shard_map/dot_general | solution.py:432
  241.1 4.0 fusion.32
  245.1 3.4 reshape.283
  248.5 5.9 %all-to-all-start.3 = ((bf16[32,20,1024]{2,1,0:T(8,128)(2,1)}), bf16[32,20,1024]{2,1,0:T(8,128)(2,1)}, u32[]{:S(2)}, u32[]{:S(2)}) async-start(bf16[32,20,1024]{2,1,0:T(8,128)(2,1)} %reshape.283), calls=%async_computation.3 | async-start | bytes 3145728 | tf_op jit(solution)/shard_map/all_to_all | solution.py:133
  255.7 7.8 %convolution_convert_fusion.1 = bf16[2048,1024]{1,0:T(8,128)(2,1)} fusion(bf16[640,2048]{1,0:T(8,128)(2,1)} %copy-done.48, bf16[640,1024]{1,0:T(8,128)(2,1)} %copy-done.21), kind=kOutput, calls=%fused_computation.48 | convolution fusion | flops 2686451712 | bytes 8126464 | tf_op jit(solution)/shard_map/dot_general | solution.py:434
  263.5 5.1 %convolution_convert_fusion.2 = bf16[1024,2048]{1,0:T(8,128)(2,1)} fusion(bf16[640,1024]{1,0:T(8,128)(2,1)S(1)} %copy-done.20, bf16[640,2048]{1,0:T(8,128)(2,1)S(1)} %copy-done.47), kind=kOutput, calls=%fused_computation.49 | convolution fusion | flops 2686451712 | bytes 8126464 | tf_op jit(solution)/shard_map/dot_general | solution.py:435
  268.6 7.3 %all-to-all-done.3 = bf16[32,20,1024]{2,1,0:T(8,128)(2,1)} async-done(((bf16[32,20,1024]{2,1,0:T(8,128)(2,1)}), bf16[32,20,1024]{2,1,0:T(8,128)(2,1)}, u32[]{:S(2)}, u32[]{:S(2)}) %all-to-all-start.3) | async-done | bytes 1310752 | tf_op jit(solution)/shard_map/all_to_all | solution.py:133
  278.2 2.8 gather_fusion.4
  281.0 3.9 reshape.299
  284.9 5.1 %reduce_sum.180 = f32[256,1024]{1,0:T(8,128)} reduce(f32[256,2,1024]{2,1,0:T(2,128)} %reshape.299, f32[]{:T(128)} %constant.33.clone.1), dimensions={1}, to_apply=%region_15.16 | reduce | flops 262144 | bytes 3145732 | tf_op jit(solution)/shard_map/reduce_sum | solution.py:440
  299.3 4.1 copy.102
  303.4 4.1 convolution_convert_fusion.4
  310.0 5.0 %fusion.9 = (f32[4,32,64]{2,1,0:T(8,128)S(1)}, bf16[4,32,64,64]{2,3,1,0:T(8,128)(2,1)S(1)}) fusion(f32[4,32,64]{2,1,0:T(8,128)S(1)} %copy-done.36, f32[4,32,64]{2,1,0:T(8,128)S(1)} %copy-done.23, f32[32,64,64]{1,2,0:T(8,128)S(1)} %copy-done.4, f32[4,32,64,64]{2,3,1,0:T(8,128)} %copy-done.1, pred[4,64,64]{1,2,0:T(8,128)(4,1)S(1)} %bitcast.190, ...), kind=kOutput, calls=%fused_computation.33 | convolution fusion | flops 38264832 | bytes 4833280 | tf_op jit(solution)/shard_map/transpose(jvp(bhqk,bkhd->bqhd))/dot_general | solution.py:97
  315.0 2.9 fusion.77
  332.4 4.5 convolution_bitcast_fusion
  336.9 7.7 %maximum_convert_fusion = bf16[1024,4096]{0,1:T(8,128)(2,1)} fusion(bf16[1024,1024]{0,1:T(8,128)(2,1)} %fusion.74, bf16[1024,3072]{0,1:T(8,128)(2,1)} %convolution_bitcast_fusion), kind=kLoop, calls=%fused_computation.7 | loop fusion | flops 16777216 | bytes 16777216 | tf_op jit(solution)/shard_map/convert.20
  344.6 11.7 %copy.111 = bf16[1024,4096]{1,0:T(8,128)(2,1)} copy(bf16[1024,4096]{0,1:T(8,128)(2,1)} %maximum_convert_fusion) | data formatting | bytes 16777216 | tf_op jit(solution)/shard_map/convert.20
  356.2 5.2 %fusion.82 = (bf16[128,8,2048]{2,1,0:T(8,128)(2,1)S(1)}, bf16[128,8,2048]{2,1,0:T(8,128)(2,1)}) fusion(bf16[128,8,4096]{2,1,0:T(8,128)(2,1)} %bitcast.148), kind=kLoop, calls=%fused_computation.174 | loop fusion | bytes 16777216 | tf_op jit(solution)/shard_map/slice | solution.py:362
  361.4 7.0 %pad_maximum_fusion.1 = bf16[128,16,2048]{2,1,0:T(8,128)(2,1)} fusion(bf16[128,8,2048]{2,1,0:T(8,128)(2,1)} %get-tuple-element.26, bf16[128,8,2048]{2,1,0:T(8,128)(2,1)S(1)} %get-tuple-element.25), kind=kLoop, calls=%fused_computation.9 | loop fusion | flops 16777216 | bytes 16777216 | tf_op jit(solution)/shard_map/concatenate | solution.py:362
  368.4 8.1 %pad_maximum_fusion.shared = bf16[4,4,2,4,16,2176]{5,4,3,2,1,0:T(8,128)(2,1)} fusion(bf16[4,4,2,4,16,128]{5,4,3,2,1,0:T(8,128)(2,1)} %bitcast.173, bf16[4,4,2,4,16,2048]{5,4,3,2,1,0:T(8,128)(2,1)} %bitcast.149), kind=kLoop, calls=%fused_computation.8 | loop fusion | flops 17825792 | bytes 17825792 | tf_op jit(solution)/shard_map/concatenate | solution.py:363
  376.5 82.8 %shard_map.198 = (f32[16,2176]{1,0:T(8,128)}, bf16[256,2048]{1,0:T(8,128)(2,1)}, bf16[512,1024]{1,0:T(8,128)(2,1)}) custom-call(bf16[4,4,2,4,16,2176]{5,4,3,2,1,0:T(8,128)(2,1)} %pad_maximum_fusion.shared, bf16[4,256,2048]{2,1,0:T(8,128)(2,1)} %bitcast.170, bf16[4,512,1024]{2,1,0:T(8,128)(2,1)} %bitcast.169), custom_call_target="tpu_custom_call" | custom-call | tf_op jit(solution)/shard_map/pallas_call | solution.py:321
  (209 shorter events, 85.6 us)
Async XLA Ops:
  0.6 60.4 %copy-start = (bf16[1024,1024]{1,0:T(8,128)(2,1)S(1)}, bf16[1024,1024]{1,0:T(8,128)(2,1)}, u32[]{:S(2)}) copy-start(bf16[1024,1024]{1,0:T(8,128)(2,1)} %param.17) | copy-start | bytes 6291460
  2.6 5.7 %copy-start.39 = (s32[4096]{0:T(1024)S(1)}, s32[4096]{0:T(1024)}, u32[]{:S(2)}) copy-start(s32[4096]{0:T(1024)} %constant.185) | copy-start | bytes 49156
  17.9 17.2 %copy-start.27 = (pred[4,64,64]{1,2,0:T(32,128)(4,1)S(1)}, pred[4,64,64]{1,2,0:T(32,128)(4,1)}, u32[]{:S(2)}) copy-start(pred[4,64,64]{1,2,0:T(32,128)(4,1)} %constant.149.clone) | copy-start | bytes 49156
  35.1 4.7 %copy-start.3 = (f32[32,64,64]{1,2,0:T(8,128)}, f32[32,64,64]{1,2,0:T(8,128)S(1)}, u32[]{:S(2)}) copy-start(f32[32,64,64]{1,2,0:T(8,128)S(1)} %copy.92) | copy-start | bytes 1572868
  38.3 5.9 %copy-start.1 = (f32[4,32,64,64]{2,3,1,0:T(8,128)}, f32[4,32,64,64]{2,3,1,0:T(8,128)S(1)}, u32[]{:S(2)}) copy-start(f32[4,32,64,64]{2,3,1,0:T(8,128)S(1)} %get-tuple-element.40) | copy-start | bytes 6291460
  38.3 5.9 %copy-start.22 = (f32[4,32,64]{2,1,0:T(8,128)}, f32[4,32,64]{2,1,0:T(8,128)S(1)}, u32[]{:S(2)}) copy-start(f32[4,32,64]{2,1,0:T(8,128)S(1)} %get-tuple-element.39) | copy-start | bytes 98308
  39.8 167.2 %copy-start.24 = (f32[4,32,64]{2,1,0:T(8,128)}, f32[4,32,64]{2,1,0:T(8,128)S(1)}, u32[]{:S(2)}) copy-start(f32[4,32,64]{2,1,0:T(8,128)S(1)} %fusion.76) | copy-start | bytes 98308
  39.8 5.8 %copy-start.14 = (bf16[4,64,1024]{1,2,0:T(8,128)(2,1)S(1)}, bf16[4,64,1024]{1,2,0:T(8,128)(2,1)}, u32[]{:S(2)}) copy-start(bf16[4,64,1024]{1,2,0:T(8,128)(2,1)} %copy.88) | copy-start | bytes 1572868
  44.2 1.4 copy-start.7
  53.5 9.3 %copy-start.15 = (bf16[256,1024]{1,0:T(8,128)(2,1)S(1)}, bf16[256,1024]{1,0:T(8,128)(2,1)}, u32[]{:S(2)}) copy-start(bf16[256,1024]{1,0:T(8,128)(2,1)} %param.15) | copy-start | bytes 1572868
  53.6 9.3 %copy-start.37 = (f32[1024]{0:T(1024)S(1)}, f32[1024]{0:T(1024)}, u32[]{:S(2)}) copy-start(f32[1024]{0:T(1024)} %param.19) | copy-start | bytes 12292
  53.6 9.3 %copy-start.42 = (f32[1024]{0:T(1024)S(1)}, f32[1024]{0:T(1024)}, u32[]{:S(2)}) copy-start(f32[1024]{0:T(1024)} %param.20) | copy-start | bytes 12292
  61.0 1.7 copy-start.9
  106.3 18.6 %copy-start.44 = (bf16[1,2048,1024]{2,1,0:T(8,128)(2,1)S(1)}, bf16[1,2048,1024]{2,1,0:T(8,128)(2,1)}, u32[]{:S(2)}) copy-start(bf16[1,2048,1024]{2,1,0:T(8,128)(2,1)} %param.25) | copy-start | bytes 12582916
  123.4 1.5 copy-start.48
  128.9 9.2 %copy-start.31 = (f32[1024,32]{0,1:T(8,128)S(1)}, f32[1024,32]{0,1:T(8,128)}, u32[]{:S(2)}) copy-start(f32[1024,32]{0,1:T(8,128)} %param.21) | copy-start | bytes 393220
  132.1 27.3 %all-to-all-start.1 = ((bf16[32,20,1024]{2,1,0:T(8,128)(2,1)}), bf16[32,20,1024]{2,1,0:T(8,128)(2,1)}, u32[]{:S(2)}, u32[]{:S(2)}) async-start(bf16[32,20,1024]{2,1,0:T(8,128)(2,1)} %reshape.279), calls=%async_computation.1 | async-start | bytes 3145728 | tf_op jit(solution)/shard_map/all_to_all | solution.py:133
  139.7 23.0 %copy-start.29 = (f32[256,1,2]{2,1,0:T(1,128)}, f32[256,1,2]{2,1,0:T(1,128)S(1)}, u32[]{:S(2)}) copy-start(f32[256,1,2]{2,1,0:T(1,128)S(1)} %fusion.55) | copy-start | bytes 6148
  167.7 9.8 %copy-start.8 = (bf16[256,1024]{1,0:T(8,128)(2,1)S(1)}, bf16[256,1024]{1,0:T(8,128)(2,1)}, u32[]{:S(2)}) copy-start(bf16[256,1024]{1,0:T(8,128)(2,1)} %param.27) | copy-start | bytes 1572868
  167.7 9.8 %copy-start.38 = (f32[1024]{0:T(1024)S(1)}, f32[1024]{0:T(1024)}, u32[]{:S(2)}) copy-start(f32[1024]{0:T(1024)} %param.22) | copy-start | bytes 12292
  167.7 10.7 %copy-start.43 = (f32[1024]{0:T(1024)S(1)}, f32[1024]{0:T(1024)}, u32[]{:S(2)}) copy-start(f32[1024]{0:T(1024)} %param.23) | copy-start | bytes 12292
  200.8 27.6 %all-to-all-start.2 = ((bf16[32,20,1024]{2,1,0:T(8,128)(2,1)}), bf16[32,20,1024]{2,1,0:T(8,128)(2,1)}, u32[]{:S(2)}, u32[]{:S(2)}) async-start(bf16[32,20,1024]{2,1,0:T(8,128)(2,1)} %broadcast_select_fusion), calls=%async_computation.2 | async-start | bytes 3145728 | tf_op jit(solution)/shard_map/all_to_all | solution.py:133
  207.0 9.3 %copy-start.30 = (f32[256,1,2]{2,1,0:T(1,128)S(1)}, f32[256,1,2]{2,1,0:T(1,128)}, u32[]{:S(2)}) copy-start(f32[256,1,2]{2,1,0:T(1,128)} %copy-done.29) | copy-start | bytes 6148
  230.7 8.9 %copy-start.21 = (bf16[640,1024]{1,0:T(8,128)(2,1)}, bf16[640,1024]{1,0:T(8,128)(2,1)S(1)}, u32[]{:S(2)}) copy-start(bf16[640,1024]{1,0:T(8,128)(2,1)S(1)} %reshape.282) | copy-start | bytes 3932164
  230.7 10.5 %copy-start.45 = (bf16[1,1024,2048]{2,1,0:T(8,128)(2,1)S(1)}, bf16[1,1024,2048]{2,1,0:T(8,128)(2,1)}, u32[]{:S(2)}) copy-start(bf16[1,1024,2048]{2,1,0:T(8,128)(2,1)} %param.24) | copy-start | bytes 12582916
  239.6 1.5 copy-start.46
  248.5 27.4 %all-to-all-start.3 = ((bf16[32,20,1024]{2,1,0:T(8,128)(2,1)}), bf16[32,20,1024]{2,1,0:T(8,128)(2,1)}, u32[]{:S(2)}, u32[]{:S(2)}) async-start(bf16[32,20,1024]{2,1,0:T(8,128)(2,1)} %reshape.283), calls=%async_computation.3 | async-start | bytes 3145728 | tf_op jit(solution)/shard_map/all_to_all | solution.py:133
  255.7 7.8 %copy-start.20 = (bf16[640,1024]{1,0:T(8,128)(2,1)S(1)}, bf16[640,1024]{1,0:T(8,128)(2,1)}, u32[]{:S(2)}) copy-start(bf16[640,1024]{1,0:T(8,128)(2,1)} %reshape.278) | copy-start | bytes 3932164
  255.7 7.8 %copy-start.47 = (bf16[640,2048]{1,0:T(8,128)(2,1)S(1)}, bf16[640,2048]{1,0:T(8,128)(2,1)}, u32[]{:S(2)}) copy-start(bf16[640,2048]{1,0:T(8,128)(2,1)} %copy-done.46) | copy-start | bytes 7864324
  281.0 8.9 %copy-start.6 = (f32[256,1024]{1,0:T(8,128)S(1)}, f32[256,1024]{1,0:T(8,128)}, u32[]{:S(2)}) copy-start(f32[256,1024]{1,0:T(8,128)} %copy-done.5) | copy-start | bytes 3145732
  281.0 8.9 %copy-start.32 = (f32[1024,32]{0,1:T(8,128)S(1)}, f32[1024,32]{0,1:T(8,128)}, u32[]{:S(2)}) copy-start(f32[1024,32]{0,1:T(8,128)} %param.21) | copy-start | bytes 393220
  281.0 8.9 %copy-start.34 = (f32[256,1,32]{2,1,0:T(1,128)S(1)}, f32[256,1,32]{2,1,0:T(1,128)}, u32[]{:S(2)}) copy-start(f32[256,1,32]{2,1,0:T(1,128)} %copy-done.33) | copy-start | bytes 98308
  281.0 11.5 %copy-start.41 = (f32[256]{0:T(256)S(1)}, f32[256]{0:T(256)}, u32[]{:S(2)}) copy-start(f32[256]{0:T(256)} %copy-done.40) | copy-start | bytes 3076
  299.3 10.6 %copy-start.4 = (f32[32,64,64]{1,2,0:T(8,128)S(1)}, f32[32,64,64]{1,2,0:T(8,128)}, u32[]{:S(2)}) copy-start(f32[32,64,64]{1,2,0:T(8,128)} %copy-done.3) | copy-start | bytes 1572868
  299.3 10.6 %copy-start.23 = (f32[4,32,64]{2,1,0:T(8,128)S(1)}, f32[4,32,64]{2,1,0:T(8,128)}, u32[]{:S(2)}) copy-start(f32[4,32,64]{2,1,0:T(8,128)} %copy-done.22) | copy-start | bytes 98308
  299.3 10.6 %copy-start.28 = (pred[4,64,64]{1,2,0:T(32,128)(4,1)S(1)}, pred[4,64,64]{1,2,0:T(32,128)(4,1)}, u32[]{:S(2)}) copy-start(pred[4,64,64]{1,2,0:T(32,128)(4,1)} %constant.149.clone) | copy-start | bytes 49156
  299.3 10.6 %copy-start.36 = (f32[4,32,64]{2,1,0:T(8,128)S(1)}, f32[4,32,64]{2,1,0:T(8,128)}, u32[]{:S(2)}) copy-start(f32[4,32,64]{2,1,0:T(8,128)} %multiply_divide_fusion) | copy-start | bytes 98308
  309.9 5.0 %copy-start.2 = (f32[4,32,64,64]{2,3,1,0:T(8,128)S(1)}, f32[4,32,64,64]{2,3,1,0:T(8,128)}, u32[]{:S(2)}) copy-start(f32[4,32,64,64]{2,3,1,0:T(8,128)} %copy-done.1) | copy-start | bytes 6291460
  309.9 5.0 %copy-start.25 = (f32[4,32,64]{2,1,0:T(8,128)S(1)}, f32[4,32,64]{2,1,0:T(8,128)}, u32[]{:S(2)}) copy-start(f32[4,32,64]{2,1,0:T(8,128)} %copy-done.24) | copy-start | bytes 98308
  315.0 2.9 copy-start.35
  315.0 3.0 copy-start.12
  315.0 3.0 copy-start.26
  317.9 2.2 copy-start.11
  320.1 6.1 %copy-start.19 = (bf16[4,64,1024]{2,1,0:T(8,128)(2,1)S(1)}, bf16[4,64,1024]{2,1,0:T(8,128)(2,1)}, u32[]{:S(2)}) copy-start(bf16[4,64,1024]{2,1,0:T(8,128)(2,1)} %copy.104) | copy-start | bytes 1572868
  326.2 2.4 slice-start
  327.8 1.2 copy-start.18
  327.8 1.9 slice-start.1
  329.7 2.6 copy-start.16
  (6 other events, 5.8 us)
